TPU v7x, 256 devices: a whole 4x4x8 slice. The times are simulated.
256 devices in a mesh: snap: 16 (over z, core), vtx: 16 (over y, x).
Axes of the slice: x: 4, y: 4, z: 8, core: 2. Of those that a mesh axis runs over, the one named last changes fastest.
Arguments:
- feats: float32 [16, 16384, 512], P('snap', 'vtx'), may hold values from -6 to 6
- col_ids: int32 [16, 128, 16], P('snap', 'vtx'), may hold values from 0 to 127
- tiles: float32 [16, 128, 16, 128, 128], P('snap', 'vtx'), may hold values from -0.125 to 0.125
- w_first: float32 [512, 256], replicated, may hold values from -0.25 to 0.25
- w_input: float32 [256, 1024], replicated, may hold values from -0.375 to 0.375
- w_recur: float32 [256, 1024], replicated, may hold values from -0.375 to 0.375
- lstm_bias: float32 [1024], replicated, may hold values from -3 to 3
- w_second: float32 [256, 256], replicated, may hold values from -0.375 to 0.375
Outputs:
- output: float32 [16, 16384, 256], P('snap', 'vtx')
Inputs may be any that keep to these rules, and one draw needn't show every extreme that they name: `col_ids`: every entry names a row block of the same snapshot's graph; a few blocks are named far more often than others.
All inputs are finite; a program needn't handle non-finite values.
Results may differ from a plain program's by a relative error of at most 0.0003.
Values sent between devices are 32-bit elements; how exact they have to be, the bound alone decides.
A program may use at most 128 MiB of HBM per device.

v0:
```python
import jax
import jax.numpy as jnp
from jax import lax
from jax.sharding import PartitionSpec as P


def block_sum(tile_set, column_ids, source):
    tile_edge = tile_set.shape[-1]
    width = source.shape[-1]
    blocks = source.reshape(source.shape[0] // tile_edge, tile_edge, width)

    def row_block(operands):
        tiles_here, ids_here = operands
        picked = blocks[ids_here]
        return jnp.einsum("ktu,kuw->tw", tiles_here, picked, precision=lax.Precision.HIGHEST)

    summed = lax.map(row_block, (tile_set, column_ids))
    return summed.reshape(-1, width)


def row_scale(tiles):
    sums = jnp.sum(tiles * tiles, axis=(2, 4))
    return lax.rsqrt(1.0 + sums).reshape(tiles.shape[0], -1)[..., None]


def recurrence(pre_time, w_recur, lstm_bias):
    hidden_size = w_recur.shape[0]

    def advance(carry, pre_step):
        state_h, state_c = carry
        gates = pre_step + jnp.dot(state_h, w_recur, precision=lax.Precision.HIGHEST) + lstm_bias
        gate_i = gates[:, :hidden_size]
        gate_f = gates[:, hidden_size : 2 * hidden_size]
        gate_g = gates[:, 2 * hidden_size : 3 * hidden_size]
        gate_o = gates[:, 3 * hidden_size :]
        state_c = jax.nn.sigmoid(gate_f) * state_c + jax.nn.sigmoid(gate_i) * jnp.tanh(gate_g)
        state_h = jax.nn.sigmoid(gate_o) * jnp.tanh(state_c)
        return ((state_h, state_c), state_h)

    zeros = jnp.zeros((pre_time.shape[1], hidden_size), jnp.float32)
    _, states = lax.scan(advance, (zeros, zeros), pre_time)
    return states


def on_device(feats, col_ids, tiles, w_first, w_input, w_recur, lstm_bias, w_second):
    scale = row_scale(tiles)
    whole = lax.all_gather(feats, "vtx", axis=1, tiled=True)
    mixed = scale * (feats + jax.vmap(block_sum)(tiles, col_ids, whole))
    hidden_one = jax.nn.relu(
        jnp.einsum("svf,fh->svh", mixed, w_first, precision=lax.Precision.HIGHEST)
    )
    timelines = lax.all_to_all(hidden_one, "snap", split_axis=1, concat_axis=0, tiled=True)
    pre_time = jnp.einsum("svh,hg->svg", timelines, w_input, precision=lax.Precision.HIGHEST)
    states = recurrence(pre_time, w_recur, lstm_bias)
    returned = lax.all_to_all(states, "snap", split_axis=0, concat_axis=1, tiled=True)
    whole_two = lax.all_gather(returned, "vtx", axis=1, tiled=True)
    mixed_two = scale * (returned + jax.vmap(block_sum)(tiles, col_ids, whole_two))
    return jnp.einsum("svh,hg->svg", mixed_two, w_second, precision=lax.Precision.HIGHEST)


def solution(mesh):
    placed = (
        P("snap", "vtx", None),
        P("snap", "vtx", None),
        P("snap", "vtx", None, None, None),
        P(),
        P(),
        P(),
        P(),
        P(),
    )
    return jax.shard_map(
        on_device, mesh=mesh, in_specs=placed, out_specs=P("snap", "vtx", None), check_vma=False
    )
```

profile of v0, /device:TPU:1, one launch (start us, length us, event | category | flops | bytes accessed | tf_op | source)
XLA Modules:
  0.0 617.5 jit_solution(13330983946178340313)
XLA Ops:
  7.3 4.0 multiply_reduce_fusion
  11.3 204.4 %all-gather.3.cloned.1.call-done = f32[1,16384,512]{2,1,0:T(8,128)} async-done(((f32[1,1024,512]{2,1,0:T(8,128)}), f32[1,16384,512]{2,1,0:T(8,128)}) %all-gather.3.cloned.1.call-update) | async-done | bytes 33554448 | tf_op jit(solution)/shard_map/all_gather | solution.py:47
  215.7 91.2 %while.35 = (s32[]{:T(128)}, f32[8,1,128,512]{3,2,1,0:T(8,128)}, f32[8,1,16,128,128]{4,3,2,1,0:T(8,128)}, s32[8,1,16]{2,1,0:T(1,128)}, f32[1,128,128,512]{3,2,1,0:T(8,128)}, /*index=5*/s32[]{:T(128)}) while((s32[]{:T(128)}, f32[8,1,128,512]{3,2,1,0:T(8,128)}, f32[8,1,16,128,128]{4,3,2,1,0:T(8,128)}, s32[8,1,16]{2,1,0:T(1,128)}, ...), condition=%wide.region_2.3_spmd, body=%wide.region_1.2_spmd.sunk | while | flops 1610612864 | bytes 13895369 | solution.py:17
  216.5 5.1 gather_fusion
  221.6 5.7 fusion.62
  227.9 5.0 gather_fusion
  232.9 5.7 fusion.62
  239.3 5.0 gather_fusion
  244.3 5.7 fusion.62
  250.6 5.1 gather_fusion
  255.7 5.7 fusion.62
  262.1 5.1 gather_fusion
  267.2 5.6 fusion.62
  273.5 5.1 gather_fusion
  278.6 5.6 fusion.62
  284.9 5.0 gather_fusion
  289.9 5.6 fusion.62
  296.2 5.0 gather_fusion
  301.2 5.7 fusion.62
  306.9 3.5 fusion.35
  310.4 2.0 copy.12
  312.5 7.8 %all-to-all-start = ((f32[1,1024,256]{2,0,1:T(1,128)}), f32[1,1024,256]{2,0,1:T(1,128)S(1)}, u32[]{:S(2)}, u32[]{:S(2)}) async-start(f32[1,1024,256]{2,0,1:T(1,128)} %copy.12), calls=%async_computation | async-start | bytes 2097152 | tf_op jit(solution)/shard_map/all_to_all | solution.py:52
  320.4 27.9 %all-to-all-done = f32[1,1024,256]{2,0,1:T(1,128)S(1)} async-done(((f32[1,1024,256]{2,0,1:T(1,128)}), f32[1,1024,256]{2,0,1:T(1,128)S(1)}, u32[]{:S(2)}, u32[]{:S(2)}) %all-to-all-start) | async-done | bytes 1048608 | tf_op jit(solution)/shard_map/all_to_all | solution.py:52
  348.3 5.0 fusion.39
  353.3 29.0 %while.37 = (s32[]{:T(128)}, f32[64,256]{1,0:T(8,128)S(1)}, f32[64,256]{1,0:T(8,128)S(1)}, f32[16,64,256]{2,1,0:T(8,128)S(1)}, f32[16,64,1024]{2,1,0:T(8,128)}, ...) while((s32[]{:T(128)}, f32[64,256]{1,0:T(8,128)S(1)}, ...), condition=%wide.region_4.5_spmd.clone, body=%wide.region_3.4_spmd.clone.sunk | while | flops 201703424 | bytes 2166896 | solution.py:41
  355.1 1.7 fusion.68
  378.8 1.7 fusion.68
  382.4 32.0 %all_to_all.27 = f32[16,64,256]{2,1,0:T(8,128)} all-to-all(f32[16,64,256]{2,1,0:T(8,128)S(1)} %get-tuple-element.97), channel_id=1, replica_groups=mesh['snap'=16,'vtx'=16] {'snap'}, dimensions={0} | all-to-all | bytes 2097152 | tf_op jit(solution)/shard_map/all_to_all | solution.py:55
  414.4 111.3 %all-gather.5.cloned.1.call-done = f32[1,16384,256]{2,1,0:T(8,128)} async-done(((f32[1,1024,256]{2,1,0:T(8,128)}), f32[1,16384,256]{2,1,0:T(8,128)}) %all-gather.5.cloned.1.call-update) | async-done | bytes 16777232 | tf_op jit(solution)/shard_map/all_gather | solution.py:56
  525.7 81.2 %while.36 = (s32[]{:T(128)}, f32[8,1,128,256]{3,2,1,0:T(8,128)}, f32[8,1,16,128,128]{4,3,2,1,0:T(8,128)}, s32[8,1,16]{2,1,0:T(1,128)}, f32[1,128,128,256]{3,2,1,0:T(8,128)}, /*index=5*/s32[]{:T(128)}) while((s32[]{:T(128)}, f32[8,1,128,256]{3,2,1,0:T(8,128)}, f32[8,1,16,128,128]{4,3,2,1,0:T(8,128)}, s32[8,1,16]{2,1,0:T(1,128)}, ...), condition=%wide.region_6.7_spmd, body=%wide.region_5.6_spmd.sunk | while | flops 805306496 | bytes 7472841 | solution.py:17
  526.4 6.4 %gather_fusion.1 = f32[16,128,256]{2,1,0:T(8,128)S(1)} fusion(f32[1,128,128,256]{3,2,1,0:T(8,128)} %get-tuple-element.352, s32[16]{0:T(128)S(1)} %or_bitcast_fusion.5), kind=kCustom, calls=%fused_computation.1.clone.1 | custom fusion | bytes 4194432 | tf_op jit(solution)/shard_map/vmap()/while/body/eval_jaxpr/gather | solution.py:14
  532.8 3.0 fusion.65
  536.5 6.4 %gather_fusion.1 = f32[16,128,256]{2,1,0:T(8,128)S(1)} fusion(f32[1,128,128,256]{3,2,1,0:T(8,128)} %get-tuple-element.352, s32[16]{0:T(128)S(1)} %or_bitcast_fusion.5), kind=kCustom, calls=%fused_computation.1.clone.1 | custom fusion | bytes 4194432 | tf_op jit(solution)/shard_map/vmap()/while/body/eval_jaxpr/gather | solution.py:14
  543.0 3.0 fusion.65
  546.7 6.4 %gather_fusion.1 = f32[16,128,256]{2,1,0:T(8,128)S(1)} fusion(f32[1,128,128,256]{3,2,1,0:T(8,128)} %get-tuple-element.352, s32[16]{0:T(128)S(1)} %or_bitcast_fusion.5), kind=kCustom, calls=%fused_computation.1.clone.1 | custom fusion | bytes 4194432 | tf_op jit(solution)/shard_map/vmap()/while/body/eval_jaxpr/gather | solution.py:14
  553.1 3.0 fusion.65
  556.8 6.4 %gather_fusion.1 = f32[16,128,256]{2,1,0:T(8,128)S(1)} fusion(f32[1,128,128,256]{3,2,1,0:T(8,128)} %get-tuple-element.352, s32[16]{0:T(128)S(1)} %or_bitcast_fusion.5), kind=kCustom, calls=%fused_computation.1.clone.1 | custom fusion | bytes 4194432 | tf_op jit(solution)/shard_map/vmap()/while/body/eval_jaxpr/gather | solution.py:14
  563.3 3.0 fusion.65
  567.0 6.4 %gather_fusion.1 = f32[16,128,256]{2,1,0:T(8,128)S(1)} fusion(f32[1,128,128,256]{3,2,1,0:T(8,128)} %get-tuple-element.352, s32[16]{0:T(128)S(1)} %or_bitcast_fusion.5), kind=kCustom, calls=%fused_computation.1.clone.1 | custom fusion | bytes 4194432 | tf_op jit(solution)/shard_map/vmap()/while/body/eval_jaxpr/gather | solution.py:14
  573.4 3.0 fusion.65
  577.1 6.4 %gather_fusion.1 = f32[16,128,256]{2,1,0:T(8,128)S(1)} fusion(f32[1,128,128,256]{3,2,1,0:T(8,128)} %get-tuple-element.352, s32[16]{0:T(128)S(1)} %or_bitcast_fusion.5), kind=kCustom, calls=%fused_computation.1.clone.1 | custom fusion | bytes 4194432 | tf_op jit(solution)/shard_map/vmap()/while/body/eval_jaxpr/gather | solution.py:14
  583.6 3.0 fusion.65
  587.3 6.4 %gather_fusion.1 = f32[16,128,256]{2,1,0:T(8,128)S(1)} fusion(f32[1,128,128,256]{3,2,1,0:T(8,128)} %get-tuple-element.352, s32[16]{0:T(128)S(1)} %or_bitcast_fusion.5), kind=kCustom, calls=%fused_computation.1.clone.1 | custom fusion | bytes 4194432 | tf_op jit(solution)/shard_map/vmap()/while/body/eval_jaxpr/gather | solution.py:14
  593.7 3.0 fusion.65
  597.4 6.4 %gather_fusion.1 = f32[16,128,256]{2,1,0:T(8,128)S(1)} fusion(f32[1,128,128,256]{3,2,1,0:T(8,128)} %get-tuple-element.352, s32[16]{0:T(128)S(1)} %or_bitcast_fusion.5), kind=kCustom, calls=%fused_computation.1.clone.1 | custom fusion | bytes 4194432 | tf_op jit(solution)/shard_map/vmap()/while/body/eval_jaxpr/gather | solution.py:14
  603.9 3.0 fusion.65
  606.9 1.8 fusion.38
  608.7 2.0 convolution_bitcast_fusion.2
  (99 shorter events, 37.1 us)
Async XLA Ops:
  6.5 341.8 %copy-start = (f32[256,1024]{1,0:T(8,128)S(1)}, f32[256,1024]{1,0:T(8,128)}, u32[]{:S(2)}) copy-start(f32[256,1024]{1,0:T(8,128)} %param.18) | copy-start | bytes 3145732
  6.5 209.2 %all-gather.3.cloned.1.call-start = ((), (), s32[]{:S(2)}) async-start(), calls=%async_computation.2 | async-start | bytes 35651584 | tf_op jit(solution)/shard_map/all_gather | solution.py:47
  215.7 91.2 %copy-start.2 = (f32[1,1024,512]{2,1,0:T(8,128)S(1)}, f32[1,1024,512]{2,1,0:T(8,128)}, u32[]{:S(2)}) copy-start(f32[1,1024,512]{2,1,0:T(8,128)} %param.14) | copy-start | bytes 6291460
  312.5 35.7 %all-to-all-start = ((f32[1,1024,256]{2,0,1:T(1,128)}), f32[1,1024,256]{2,0,1:T(1,128)S(1)}, u32[]{:S(2)}, u32[]{:S(2)}) async-start(f32[1,1024,256]{2,0,1:T(1,128)} %copy.12), calls=%async_computation | async-start | bytes 2097152 | tf_op jit(solution)/shard_map/all_to_all | solution.py:52
  320.3 205.4 %all-gather.5.cloned.1.call-start = ((), (), s32[]{:S(2)}) async-start(), calls=%async_computation.3 | async-start | bytes 17825792 | tf_op jit(solution)/shard_map/all_gather | solution.py:56
  348.3 5.0 copy-start.1
  348.3 5.0 copy-start.4
  606.9 1.8 copy-start.3
Sparse Core Ops, SparseCore 0:
  9.8 205.8 all-gather.2
  414.5 111.1 all-gather.4
where the time goes:
time: 619 us; the launch traced here: 617 us
  waiting for transfers between devices  344 us (56%)
  matrix products  107 us (17%)
  local copies, waits for them, and re-layouts  94.3 us (15%)
  blocking collectives  32 us (5%)
  other arithmetic  18 us (3%)
  between operations  13.5 us (2%)
  starting transfers between devices  7.85 us (1%)
    all_gather x1, waiting for transfers between devices, on_device(): whole = lax.all_gather(feats, 'vtx', axis=1, tiled=True)  204 us
    all_gather x1, waiting for transfers between devices, on_device(): whole_two = lax.all_gather(returned, 'vtx', axis=1, tiled=True)  111 us
    gather x32, local copies, waits for them, and re-layouts, row_block(): picked = blocks[ids_here]  92.1 us
    dot_general x16, matrix products, row_block(): jnp.einsum('ktu,kuw->tw', tiles_here, picked, precision=lax.Precision.HIG...  69.3 us
    all_to_all x1, blocking collectives, on_device(): lax.all_to_all(states, 'snap', split_axis=0, concat_axis=1, tiled=True)  32 us
    all_to_all x1, waiting for transfers between devices, on_device(): lax.all_to_all(hidden_one, 'snap', split_axis=1, concat_axis=0, tiled=True)  27.9 us
    dot_general x16, matrix products, advance(): jnp.dot(state_h, w_recur, precision=lax.Precision.HIGHEST)  27.3 us
  transfers between devices with their start and end apart: 3, of which 3 were waited for; matrix products, arithmetic and copies ran while one was open for 1% of the time, Pallas kernels for 0%

commit v1 on v0

--- a/solution.py
+++ b/solution.py
@@ -44,7 +44,9 @@
 
 def on_device(feats, col_ids, tiles, w_first, w_input, w_recur, lstm_bias, w_second):
     scale = row_scale(tiles)
-    whole = lax.all_gather(feats, "vtx", axis=1, tiled=True)
+    whole = jnp.concatenate(
+        lax.all_to_all(jnp.stack([feats] * lax.axis_size("vtx")), "vtx", 0, 0), axis=1
+    )
     mixed = scale * (feats + jax.vmap(block_sum)(tiles, col_ids, whole))
     hidden_one = jax.nn.relu(
         jnp.einsum("svf,fh->svh", mixed, w_first, precision=lax.Precision.HIGHEST)

time: 619 us -> 932 us (1.51)
  waiting for transfers between devices: 344 us -> 631 us
  starting transfers between devices: 7.85 us -> 20.9 us
  local copies, waits for them, and re-layouts: 94.3 us -> 106 us
    all_to_all x0 -> x1, waiting for transfers between devices: none -> 494 us  [on_device(): lax.all_to_all(jnp.stack([feats] * lax.axis_size('vtx')), 'vtx', 0, 0)]
    all_gather x1 -> x0, waiting for transfers between devices: 204 us -> none  [on_device(): whole = lax.all_gather(feats, 'vtx', axis=1, tiled=True)]
    another operation x0 -> x1, local copies, waits for them, and re-layouts: none -> 12.3 us  [on_device(): jnp.stack([feats] * lax.axis_size('vtx'))]
  transfers between devices with their start and end apart: 3 -> 3, of which waited for: 3 -> 3; matrix products, arithmetic and copies ran while one was open for 1% -> 0% of each run, Pallas kernels for 0% -> 0%
where the time goes in v1:
time: 932 us; the launch traced here: 930 us
  waiting for transfers between devices  631 us (68%)
  matrix products  107 us (11%)
  local copies, waits for them, and re-layouts  106 us (11%)
  blocking collectives  32 us (3%)
  starting transfers between devices  20.9 us (2%)
  other arithmetic  18 us (2%)
  between operations  13.5 us (1%)
    all_to_all x1, waiting for transfers between devices, on_device(): lax.all_to_all(jnp.stack([feats] * lax.axis_size('vtx')), 'vtx', 0, 0)  494 us
    all_gather x1, waiting for transfers between devices, on_device(): whole_two = lax.all_gather(returned, 'vtx', axis=1, tiled=True)  109 us
    gather x32, local copies, waits for them, and re-layouts, row_block(): picked = blocks[ids_here]  92.1 us
    dot_general x16, matrix products, row_block(): jnp.einsum('ktu,kuw->tw', tiles_here, picked, precision=lax.Precision.HIG...  69.4 us
    all_to_all x1, blocking collectives, on_device(): lax.all_to_all(states, 'snap', split_axis=0, concat_axis=1, tiled=True)  32 us
    all_to_all x1, waiting for transfers between devices, on_device(): lax.all_to_all(hidden_one, 'snap', split_axis=1, concat_axis=0, tiled=True)  27.9 us
    dot_general x16, matrix products, advance(): jnp.dot(state_h, w_recur, precision=lax.Precision.HIGHEST)  27.3 us
  transfers between devices with their start and end apart: 3, of which 3 were waited for; matrix products, arithmetic and copies ran while one was open for 0% of the time, Pallas kernels for 0%

profile of v1, /device:TPU:1, one launch (start us, length us, event | category | flops | bytes accessed | tf_op | source)
XLA Modules:
  0.0 929.7 jit_solution(15968206536600326492)
XLA Ops:
  6.5 12.3 %stack.2 = f32[16,1,1024,512]{3,2,1,0:T(8,128)} broadcast(f32[1024,512]{1,0:T(8,128)} %bitcast.110), dimensions={2,3} | broadcast | bytes 35651584 | tf_op jit(solution)/shard_map/stack | solution.py:48
  18.8 7.6 all-to-all-start
  26.5 4.0 multiply_reduce_fusion
  30.5 493.9 %all-to-all-done = f32[16,1,1024,512]{3,2,1,0:T(8,128)} async-done(((f32[16,1,1024,512]{3,2,1,0:T(8,128)}), f32[16,1,1024,512]{3,2,1,0:T(8,128)}, u32[]{:S(2)}, u32[]{:S(2)}) %all-to-all-start) | async-done | bytes 33554464 | tf_op jit(solution)/shard_map/all_to_all | solution.py:48
  524.4 91.2 %while.35 = (s32[]{:T(128)}, f32[8,1,128,512]{3,2,1,0:T(8,128)}, f32[8,1,16,128,128]{4,3,2,1,0:T(8,128)}, s32[8,1,16]{2,1,0:T(1,128)}, f32[1,128,128,512]{3,2,1,0:T(8,128)}, /*index=5*/s32[]{:T(128)}) while((s32[]{:T(128)}, f32[8,1,128,512]{3,2,1,0:T(8,128)}, f32[8,1,16,128,128]{4,3,2,1,0:T(8,128)}, s32[8,1,16]{2,1,0:T(1,128)}, ...), condition=%wide.region_2.3_spmd, body=%wide.region_1.2_spmd.sunk | while | flops 1610612864 | bytes 13895369 | solution.py:17
  525.2 5.0 gather_fusion
  530.2 5.7 fusion.62
  536.5 5.0 gather_fusion
  541.5 5.7 fusion.62
  547.9 5.0 gather_fusion
  552.9 5.7 fusion.62
  559.2 5.1 gather_fusion
  564.3 5.7 fusion.62
  570.6 5.1 gather_fusion
  575.7 5.7 fusion.62
  582.1 5.1 gather_fusion
  587.2 5.7 fusion.62
  593.5 5.0 gather_fusion
  598.5 5.7 fusion.62
  604.9 5.0 gather_fusion
  609.9 5.7 fusion.62
  615.5 3.5 fusion.35
  619.1 2.0 copy.12
  621.1 13.2 %all-to-all-start.1 = ((f32[1,1024,256]{2,0,1:T(1,128)}), f32[1,1024,256]{2,0,1:T(1,128)S(1)}, u32[]{:S(2)}, u32[]{:S(2)}) async-start(f32[1,1024,256]{2,0,1:T(1,128)} %copy.12), calls=%async_computation.1 | async-start | bytes 2097152 | tf_op jit(solution)/shard_map/all_to_all | solution.py:54
  634.4 27.9 %all-to-all-done.1 = f32[1,1024,256]{2,0,1:T(1,128)S(1)} async-done(((f32[1,1024,256]{2,0,1:T(1,128)}), f32[1,1024,256]{2,0,1:T(1,128)S(1)}, u32[]{:S(2)}, u32[]{:S(2)}) %all-to-all-start.1) | async-done | bytes 1048608 | tf_op jit(solution)/shard_map/all_to_all | solution.py:54
  662.4 5.0 fusion.39
  667.4 29.0 %while.37 = (s32[]{:T(128)}, f32[64,256]{1,0:T(8,128)S(1)}, f32[64,256]{1,0:T(8,128)S(1)}, f32[16,64,256]{2,1,0:T(8,128)S(1)}, f32[16,64,1024]{2,1,0:T(8,128)}, ...) while((s32[]{:T(128)}, f32[64,256]{1,0:T(8,128)S(1)}, ...), condition=%wide.region_4.5_spmd.clone, body=%wide.region_3.4_spmd.clone.sunk | while | flops 201703424 | bytes 2166896 | solution.py:41
  696.5 32.0 %all_to_all.32 = f32[16,64,256]{2,1,0:T(8,128)} all-to-all(f32[16,64,256]{2,1,0:T(8,128)S(1)} %get-tuple-element.97), channel_id=1, replica_groups=mesh['snap'=16,'vtx'=16] {'snap'}, dimensions={0} | all-to-all | bytes 2097152 | tf_op jit(solution)/shard_map/all_to_all | solution.py:57
  728.5 109.4 %all-gather.2.cloned.1.call-done = f32[1,16384,256]{2,1,0:T(8,128)} async-done(((f32[1,1024,256]{2,1,0:T(8,128)}), f32[1,16384,256]{2,1,0:T(8,128)}) %all-gather.2.cloned.1.call-update) | async-done | bytes 16777232 | tf_op jit(solution)/shard_map/all_gather | solution.py:58
  837.9 81.2 %while.36 = (s32[]{:T(128)}, f32[8,1,128,256]{3,2,1,0:T(8,128)}, f32[8,1,16,128,128]{4,3,2,1,0:T(8,128)}, s32[8,1,16]{2,1,0:T(1,128)}, f32[1,128,128,256]{3,2,1,0:T(8,128)}, /*index=5*/s32[]{:T(128)}) while((s32[]{:T(128)}, f32[8,1,128,256]{3,2,1,0:T(8,128)}, f32[8,1,16,128,128]{4,3,2,1,0:T(8,128)}, s32[8,1,16]{2,1,0:T(1,128)}, ...), condition=%wide.region_6.7_spmd, body=%wide.region_5.6_spmd.sunk | while | flops 805306496 | bytes 7472841 | solution.py:17
  838.6 6.4 gather_fusion.1
  845.0 3.0 fusion.65
  848.7 6.4 gather_fusion.1
  855.2 3.0 fusion.65
  858.9 6.4 gather_fusion.1
  865.3 3.0 fusion.65
  869.0 6.4 gather_fusion.1
  875.5 3.0 fusion.65
  879.2 6.4 gather_fusion.1
  885.6 3.0 fusion.65
  889.3 6.4 gather_fusion.1
  895.8 3.0 fusion.65
  899.5 6.4 gather_fusion.1
  905.9 3.0 fusion.65
  909.6 6.4 gather_fusion.1
  916.1 3.0 fusion.65
  919.1 1.8 fusion.38
  920.9 2.0 convolution_bitcast_fusion.2
  (99 shorter events, 39.8 us)
Async XLA Ops:
  6.5 655.8 %copy-start = (f32[256,1024]{1,0:T(8,128)S(1)}, f32[256,1024]{1,0:T(8,128)}, u32[]{:S(2)}) copy-start(f32[256,1024]{1,0:T(8,128)} %param.18) | copy-start | bytes 3145732
  18.8 505.5 %all-to-all-start = ((f32[16,1,1024,512]{3,2,1,0:T(8,128)}), f32[16,1,1024,512]{3,2,1,0:T(8,128)}, u32[]{:S(2)}, u32[]{:S(2)}) async-start(f32[16,1,1024,512]{3,2,1,0:T(8,128)} %stack.2), calls=%async_computation | async-start | bytes 67108864 | tf_op jit(solution)/shard_map/all_to_all | solution.py:48
  524.4 91.2 %copy-start.2 = (f32[1,1024,512]{2,1,0:T(8,128)S(1)}, f32[1,1024,512]{2,1,0:T(8,128)}, u32[]{:S(2)}) copy-start(f32[1,1024,512]{2,1,0:T(8,128)} %param.14) | copy-start | bytes 6291460
  621.1 41.2 %all-to-all-start.1 = ((f32[1,1024,256]{2,0,1:T(1,128)}), f32[1,1024,256]{2,0,1:T(1,128)S(1)}, u32[]{:S(2)}, u32[]{:S(2)}) async-start(f32[1,1024,256]{2,0,1:T(1,128)} %copy.12), calls=%async_computation.1 | async-start | bytes 2097152 | tf_op jit(solution)/shard_map/all_to_all | solution.py:54
  634.4 203.5 %all-gather.2.cloned.1.call-start = ((), (), s32[]{:S(2)}) async-start(), calls=%async_computation.3 | async-start | bytes 17825792 | tf_op jit(solution)/shard_map/all_gather | solution.py:58
  662.4 5.1 copy-start.1
  662.4 5.0 copy-start.4
  919.1 1.8 copy-start.3
Sparse Core Ops, SparseCore 0:
  728.6 109.2 all-gather.1
